TPU v7x, 32 devices: a whole 2x2x4 slice. The times are simulated.
32 devices in a mesh: fsdp: 32 (over z, y, x, core).
Axes of the slice: x: 2, y: 2, z: 4, core: 2. Of those that a mesh axis runs over, the one named last changes fastest.
Arguments:
- layer_in: bfloat16 [64, 416, 768], P('fsdp'), may hold values from -24 to 24
- pair_ids: int32 [64, 416], P('fsdp'), may hold values from 0 to 2, as said below
- pair_lengths: int32 [64, 3, 2], P('fsdp'), may hold values from 1 to 273, as said below
- attn_shard: bfloat16 [2363392], P('fsdp'), may hold values from -2 to 2
- ffn_shard: bfloat16 [4726784], P('fsdp'), may hold values from -2 to 2
- out_grad: bfloat16 [64, 416, 768], P('fsdp'), may hold values from -8 to 8
Outputs:
- layer_out: bfloat16 [64, 416, 768], P('fsdp')
- in_grad: float32 [64, 416, 768], P('fsdp')
- attn_grad: float32 [2363392], P('fsdp')
- ffn_grad: float32 [4726784], P('fsdp')
- out_bias_grad: float32 [768], replicated
Inputs may be any that keep to these rules, and one draw needn't show every extreme that they name: `pair_ids`: ids never decrease along a row, and every id of 0 to 2 occupies a run of slots in every row. `pair_lengths`: [.., 0] counts text slots and [.., 1] region slots; their sum is at most the pair's run of slots, and the live slots are the first ones of the run.
All inputs are finite; a program needn't handle non-finite values.
Results may differ from a plain program's by a relative error of at most 0.014.
The roundings to bfloat16 on the way count: a program that leaves them out, or rounds other values in their place, can miss the bound.
Values may be sent and summed in bfloat16 or wider, within the bound.
A program may use at most 192 MiB of HBM per device.

v0:
```python
import functools

import jax
import jax.numpy as jnp
from jax import lax
from jax.experimental import pallas as pl
from jax.experimental.pallas import tpu as pltpu
from jax.sharding import PartitionSpec as P

D = 768
HEADS = 12
HEAD_DIM = 64
FF = 3072
SLOTS = 416
PAIRS = 3
LANES = 128
NORM_EPS = 1e-12
F32 = jnp.float32
BF16 = jnp.bfloat16
MESH = pl.DeviceIdType.MESH
VMEM_LIMIT = 62 << 20
FINISH = 11
RELAY, PROJECT, ATTEND, NORM, UP, DOWN, TURN, BACK_WEIGHT, HIDDEN, LEAVE, ATTEND_BACK, JOINT, INPUT_GRAD = range(
    0, 1300, 100
)


def dot_nn(a, b):
    return lax.dot_general(a, b, (((1,), (0,)), ((), ())), preferred_element_type=F32)


def dot_nt(a, b):
    return lax.dot_general(a, b, (((1,), (1,)), ((), ())), preferred_element_type=F32)


def dot_tn(a, b):
    return lax.dot_general(a, b, (((0,), (0,)), ((), ())), preferred_element_type=F32)


def row_mean(v):
    return jnp.sum(v, axis=1, keepdims=True) * (1.0 / D)


def col_sum(v):
    return jnp.sum(v, axis=0, keepdims=True)


class Plan:
    def __init__(self, n, attn_shard_len, ffn_shard_len, row_count):
        self.n = n
        self.nz = n // 8
        self.rows = row_count
        self.tokens = row_count * SLOTS
        self.unit_a = attn_shard_len // LANES
        self.unit_f = ffn_shard_len // LANES
        self.block_a = 4 * D * D // LANES // n
        self.block_f = 2 * D * FF // LANES // n
        self.rows_a = 4 * D // n
        self.rows_f = 2 * FF // n
        self.joint_rows = self.rows_a // 3
        self.joint_src = 3 * n // 4
        self.in_rows = self.rows_f // 4
        self.in_src = n // 2
        self.part_a = (0, self.rows_a, 16, 32)
        self.part_f = (0, self.rows_f, 48, 64)
        self.gap = FF // LANES
        self.at_attn_vec = divmod(4 * D * D // LANES, self.unit_a)
        self.at_bias_in = divmod(D * FF // LANES, self.unit_f)
        self.at_ffn_vec = divmod(2 * D * FF // LANES + self.gap, self.unit_f)

    def shift_a(self, me):
        return me * (self.unit_a - self.block_a)

    def shift_f(self, me):
        return me * (self.unit_f - self.block_f) - jnp.where(me >= self.in_src, self.gap, 0)

    def fits(self):
        n = self.n
        if self.nz != 4 or n % 8 or self.rows_a % 48 or self.rows_f % 64:
            return False
        last_a = (n - 1) * (self.unit_a - self.block_a)
        step_f = self.unit_f - self.block_f
        last_f = max((self.in_src - 1) * step_f, (n - 1) * step_f - self.gap)
        first_f = self.in_src * step_f - self.gap
        self.tail_a = -(-(last_a + 1) // 8) * 8
        self.tail_f = -(-(last_f + 2) // 8) * 8
        vec_a, vec_f = 5 * D // LANES, 3 * D // LANES
        return (
            step_f >= 0
            and self.unit_a >= self.block_a
            and first_f >= 0
            and self.tail_a <= self.block_a
            and self.tail_f <= self.block_f
            and self.at_attn_vec[0] == n - 1
            and self.at_ffn_vec[0] == n - 1
            and self.at_bias_in[0] == self.in_src - 1
            and self.unit_a - self.at_attn_vec[1] <= self.tail_a
            and self.unit_f - self.at_ffn_vec[1] <= self.tail_f
            and self.at_attn_vec[1] + vec_a <= self.unit_a
            and self.at_ffn_vec[1] + vec_f <= self.unit_f
            and self.at_bias_in[1] + self.gap <= self.unit_f
            and self.at_bias_in[1] == self.block_f - (self.in_src - 1) * step_f
        )


class Place:
    def __init__(self, plan):
        self.n, self.nz = plan.n, plan.nz
        me = lax.axis_index("fsdp")
        self.me = me
        self.core = lax.rem(me, 2)
        self.x = lax.rem(me // 2, 2)
        self.y = lax.rem(me // 4, 2)
        self.z = me // 8
        self.sib = me + 1 - 2 * self.core
        self.xn = me + 2 - 4 * self.x
        self.yn = me + 4 - 8 * self.y

    def block(self, column, z, other_core=False):
        x = self.x if column in (0, 2) else 1 - self.x
        y = self.y if column in (0, 1) else 1 - self.y
        core = 1 - self.core if other_core else self.core
        return ((z * 2 + y) * 2 + x) * 2 + core

    def level(self, distance, fn):
        if distance == 0:
            fn(self.z)
            return
        pl.when(self.z >= distance)(lambda: fn(self.z - distance))
        pl.when(self.z + distance < self.nz)(lambda: fn(self.z + distance))

    def onward(self, z, fn):
        pl.when((z <= self.z) & (self.z < self.nz - 1))(lambda: fn(self.me + 8))
        pl.when((z >= self.z) & (self.z > 0))(lambda: fn(self.me - 8))

    def bits(self):
        out = []
        bit = 1
        while bit < self.n:
            out.append(self.me + bit - 2 * bit * lax.rem(self.me // bit, 2))
            bit *= 2
        return out

    def greet(self, hubs):
        sem = pltpu.get_barrier_semaphore()

        def tell(partner):
            pl.semaphore_signal(sem, inc=1, device_id=(partner,), device_id_type=MESH)

        fixed = self.bits()
        for partner in fixed:
            tell(partner)
        z_odd = lax.rem(self.z, 2)
        far_z = (self.z > 0) & (self.z < self.nz - 1)
        far = (self.me > 0) & (self.me < self.n - 1)
        pl.when(far_z)(lambda: tell(self.me - 8 + 16 * z_odd))
        pl.when(far)(lambda: tell(self.me - 1 + 2 * self.core))
        count = len(fixed) + far_z.astype(jnp.int32) + far.astype(jnp.int32)
        for hub in hubs:
            pl.when(self.me != hub)(lambda: tell(hub))
            count = count + jnp.where(self.me == hub, self.n - 1, 0)
        return lambda: pl.semaphore_wait(sem, count)


class Wire:
    def __init__(self, send, recv):
        self.send, self.recv = send, recv
        self.sent = []

    def copy(self, src, dst, number, partner):
        return pltpu.make_async_remote_copy(
            src_ref=src,
            dst_ref=dst,
            send_sem=self.send.at[number],
            recv_sem=self.recv.at[number],
            device_id=(partner,),
            device_id_type=MESH,
        )


def add_over_all(place, wire, base, own, held):
    partners = place.bits()

    def send(s):
        wire.copy(own.at[s], held.at[s], base + s, partners[s]).start()

    def take(s):
        wire.copy(own.at[s], held.at[s], base + s, partners[s]).wait()
        own[s + 1] = own[s] + held[s]

    steps = [lambda: send(0)]
    for s in range(len(partners)):

        def step(s=s):
            take(s)
            if s + 1 < len(partners):
                send(s + 1)

        steps.append(step)
    return steps


def gather_count(nz):
    return 17 * nz + 3


class Gather:
    def __init__(self, place, wire, base, ref, top, rows, late, half):
        self.p, self.w, self.ref = place, wire, ref
        nz = place.nz
        self.early = (top, rows - late)
        self.late = (top + rows - late, late)
        self.first = (top, half)
        self.second = (top + half, rows - late - half)
        at = [base]

        def take(count):
            at[0] += count
            return at[0] - count

        self.line, self.xs, self.ys, self.d1, self.d2 = (take(nz) for _ in range(5))
        self.sib, self.late_line, self.late_sib = (take(4 * nz) for _ in range(3))
        self.px, self.py, self.pd = (take(1) for _ in range(3))

    def move(self, column, z, part, number, partner):
        ref = self.ref.at[self.p.block(column, z), pl.ds(*part)]
        return self.w.copy(ref, ref, number, partner)

    def send(self, *args):
        self.move(*args).start()

    def wait(self, column, z, part, number):
        self.move(column, z, part, number, self.p.sib).wait_recv()

    def to_sib(self, column, z):
        self.send(column, z, self.early, self.sib + column * self.p.nz + z, self.p.sib)

    def spread(self, z):
        p = self.p
        p.onward(z, lambda partner: self.send(0, z, self.early, self.line + z, partner))
        self.send(0, z, self.early, self.xs + z, p.xn)
        self.send(0, z, self.early, self.ys + z, p.yn)
        self.to_sib(0, z)

    def spread_late(self, column, z):
        number = column * self.p.nz + z
        self.p.onward(
            z, lambda partner: self.send(column, z, self.late, self.late_line + number, partner)
        )
        self.send(column, z, self.late, self.late_sib + number, self.p.sib)

    def take_line(self, z):
        self.wait(0, z, self.early, self.line + z)
        self.spread(z)

    def take_x(self, z):
        self.wait(1, z, self.early, self.xs + z)
        self.send(1, z, self.first, self.d1 + z, self.p.yn)
        self.to_sib(1, z)

    def take_y(self, z):
        self.wait(2, z, self.early, self.ys + z)
        self.send(2, z, self.second, self.d2 + z, self.p.xn)
        self.to_sib(2, z)

    def take_corner(self, z):
        self.wait(3, z, self.first, self.d1 + z)
        self.wait(3, z, self.second, self.d2 + z)
        self.to_sib(3, z)

    def take_late(self, z):
        for column in range(4):
            self.wait(column, z, self.late, self.late_line + column * self.p.nz + z)
            self.spread_late(column, z)

    def begin(self):
        self.spread(self.p.z)

    def begin_late(self):
        p = self.p
        self.send(0, p.z, self.late, self.px, p.xn)
        self.send(0, p.z, self.late, self.py, p.yn)

    def late_x(self):
        self.wait(1, self.p.z, self.late, self.px)
        self.send(1, self.p.z, self.late, self.pd, self.p.yn)

    def late_y(self):
        self.wait(2, self.p.z, self.late, self.py)

    def late_corner(self):
        self.wait(3, self.p.z, self.late, self.pd)

    def step(self, kind, number):
        p = self.p
        plane, digit = number // 10, number % 10
        starts = (self.begin, self.begin_late, self.late_x, self.late_y, self.late_corner,
                  lambda: self.spread_late(digit, p.z))
        takes = (self.take_line, self.take_x, self.take_y, self.take_corner, self.take_late)
        if kind == FINISH:
            planes = range(plane, plane + digit)
            return lambda: self.finish(planes)
        if kind < len(starts):
            return lambda: pl.when(p.z == plane)(starts[kind])
        take = takes[kind - len(starts)]
        if digit:
            return lambda: pl.when((p.z == plane - digit) | (p.z == plane + digit))(lambda: take(plane))
        return lambda: take(plane)

    def finish(self, planes):
        p, nz = self.p, self.p.nz

        def one(j, carry):
            for column in range(4):
                ref = self.ref.at[p.block(column, j, True)]
                for part, base in ((self.early, self.sib), (self.late, self.late_sib)):
                    r = ref.at[pl.ds(*part)]
                    self.w.copy(r, r, base + column * nz + j, p.sib).wait_recv()
            return carry

        lax.fori_loop(planes[0], planes[-1] + 1, one, 0)

    def drain(self):
        p, nz = self.p, self.p.nz

        def sent(column, z, part, number):
            self.move(column, z, part, number, p.sib).wait_send()

        sent(0, p.z, self.late, self.px)
        sent(0, p.z, self.late, self.py)
        sent(1, p.z, self.late, self.pd)

        def one(z, carry):
            p.onward(z, lambda partner: sent(0, z, self.early, self.line + z))
            sent(0, z, self.early, self.xs + z)
            sent(0, z, self.early, self.ys + z)
            sent(1, z, self.first, self.d1 + z)
            sent(2, z, self.second, self.d2 + z)
            for column in range(4):
                number = column * nz + z
                sent(column, z, self.early, self.sib + number)
                sent(column, z, self.late, self.late_sib + number)
                p.onward(z, lambda partner: sent(column, z, self.late, self.late_line + number))
            return carry

        lax.fori_loop(0, nz, one, 0)


def gather_count(nz):
    return 17 * nz + 3


ORDER = (
    10030, 10000, 10500, 10010, 10510, 10020, 10120, 0, 10130, 10100, 20030, 20000, 20500, 20020, 20100,
    10110, 10200, 10601, 10501, 20130, 10300, 10621, 10631, 10210, 20010, 10230, 10220, 10611, 10502, 20530,
    10520, 10602, 10622, 10612, 10310, 10632, 10531, 10400, 10512, 10320, 10522, 10430, 10533, 10503, 10521,
    20520, 10603, 10420, 10523, 20200, 20120, 10410, 20501, 10513, 10810, 11002, 10511, 10330, 10633, 10820,
    10720, 11011, 10710, 11001, 10800, 20110, 20230, 10700, 10530, 20400, 20631, 11022, 11021, 10532, 20601,
    10730, 10830, 11012, 11003, 20220, 20521, 20602, 20300, 20621, 20503, 20502, 20310, 11031, 20512, 20330,
    10920, 10910, 20611, 20430, 10900, 20320, 11121, 11111, 20210, 20632, 20533, 11101, 20531, 20522, 100,
    20622, 21001, 102, 20532, 11032, 20510, 20603, 101, 103, 200, 10930, 20420, 20523, 20511, 20612, 20633,
    201, 21002, 11033, 11131, 20410, 20513, 21031, 20700, 21021, 20800, 202, 203, 20710, 20810, 20830,
    21011, 20730, 204, 20900, 20820, 21003, 21032, 205, 300, 20720, 21022, 20910, 301, 21012, 20930, 21102,
    400, 20920, 401, 21033, 21122, 402, 403, 500, 501, 502, 503, 600, 700, 30030, 701, 30020, 30230, 30130,
    30633, 800, 30220, 30120, 30622, 801, 802, 30430, 30330, 30320, 803, 30420, 30632, 804, 805, 806, 30533,
    30621, 807, 30000, 30010, 900, 30100, 901, 30200, 30110, 30603, 902, 30631, 30522, 30210, 30612, 30532,
    30300, 1000, 30400, 30410, 1001, 30602, 30310, 1002, 30630, 30503, 1101, 40001, 40002, 30611, 40003,
    30531, 30730, 1003, 30601, 40101, 30620, 30512, 30720, 40203, 30502, 40201, 40103, 40603, 30830, 1004,
    40403, 30521, 40102, 40401, 30610, 30710, 30820, 40301, 30511, 40303, 40202, 1005, 40302, 40402, 30501,
    1102, 50003, 30600, 40503, 60000, 30920, 50103, 30700, 30810, 30930, 30520, 30530, 50002, 50001, 40602,
    40000, 60001, 50203, 50603, 40502, 50102, 50303, 50403, 1200, 30800, 50101, 40100, 50202, 50602, 30510,
    60002, 50000, 50302, 40601, 30910, 50402, 50503, 50100, 30500, 30900, 50201, 40200, 50401, 50601, 50301,
    50200, 40600, 40700, 60003, 50502, 40501, 50600, 50700, 40300, 40400, 1201, 60004, 50400, 50300, 50501,
    40800, 50800, 1202, 1203, 40500, 40900, 60005, 50900, 50500,
)

class Scatter:
    def __init__(self, place, wire, base, terms, columns, top, rows, late, half, room):
        self.p, self.w, self.terms, self.columns = place, wire, terms, columns
        nz = place.nz
        self.whole = (top, rows)
        self.early = (top, rows - late)
        self.late = (top + rows - late, late)
        self.first = (top, half)
        self.second = (top + half, rows - late - half)
        (self.side, self.in_first, self.in_second, self.in_x, self.in_y, self.in_line, self.in_late,
         self.in_plane) = room
        at = [base]

        def take(count):
            at[0] += count
            return at[0] - count

        self.sib = take(4 * nz)
        self.d1, self.d2, self.xs, self.ys = (take(nz) for _ in range(4))
        self.line = take(nz + 1)
        self.late_line = take(4 * (nz + 1))
        self.plane = take(3)

    @staticmethod
    def rooms(nz, columns, top, rows, late, half):
        def room(count, size):
            return pltpu.VMEM((count, size, columns), BF16)

        early = rows - late
        return [
            room(4 * nz, rows), room(nz, half), room(nz, early - half), room(nz, early), room(nz, early),
            room(nz + 1, early), room(4 * (nz + 1), late), room(3, late),
        ]

    def slot(self, column, z):
        return column * self.p.nz + z

    def term(self, column, z, part, other_core=False):
        return self.terms.at[self.p.block(column, z, other_core), pl.ds(*part), pl.ds(*self.columns)]

    def add(self, target, term):
        count = target.shape[0]
        step = count if count <= 48 else next(s for s in (48, 32, 16) if count % s == 0)

        def some(i, carry):
            rs = pl.ds(pl.multiple_of(i * step, 16), step)
            target[rs, :] = target[rs, :] + term[rs, :]
            return carry

        lax.fori_loop(0, count // step, some, 0)

    def got(self, ref, number):
        self.w.copy(ref, ref, number, self.p.sib).wait_recv()
        return ref

    def send_sib(self, z):
        p = self.p
        for column in (3, 1, 2, 0):
            k = self.slot(column, z)
            self.w.copy(self.term(column, z, self.whole, True), self.side.at[k], self.sib + k, p.sib).start()

    def take_sib(self, column, z):
        k = self.slot(column, z)
        self.add(self.term(column, z, self.whole), self.got(self.side.at[k], self.sib + k))

    def corner(self, z):
        p = self.p
        self.take_sib(3, z)
        self.w.copy(self.term(3, z, self.first), self.in_first.at[z], self.d1 + z, p.yn).start()
        self.w.copy(self.term(3, z, self.second), self.in_second.at[z], self.d2 + z, p.xn).start()

    def take_rest(self, z):
        for column in (1, 2, 0):
            self.take_sib(column, z)

    def side_x(self, z):
        p = self.p
        self.add(self.term(1, z, self.first), self.got(self.in_first.at[z], self.d1 + z))
        self.w.copy(self.term(1, z, self.early), self.in_x.at[z], self.xs + z, p.xn).start()

    def side_y(self, z):
        p = self.p
        self.add(self.term(2, z, self.second), self.got(self.in_second.at[z], self.d2 + z))
        self.w.copy(self.term(2, z, self.early), self.in_y.at[z], self.ys + z, p.yn).start()

    def own(self, z):
        ref = self.term(0, z, self.early)
        self.add(ref, self.got(self.in_x.at[z], self.xs + z))
        self.add(ref, self.got(self.in_y.at[z], self.ys + z))
        self.along(z, ref, self.in_line, self.line, 0)

    def own_late(self, z):
        for column in range(4):
            self.along(z, self.term(column, z, self.late), self.in_late, self.late_line,
                       column * (self.p.nz + 1))

    def along(self, z, ref, room, number, at):
        p, nz = self.p, self.p.nz
        below, above = p.z > 0, p.z < nz - 1

        def take(slot):
            self.add(ref, self.got(room.at[at + slot], number + at + slot))

        def send(slot, partner):
            self.w.copy(ref, room.at[at + slot], number + at + slot, partner).start()

        pl.when((z >= p.z) & below)(lambda: take(z))
        pl.when((z < p.z) & above)(lambda: take(z))
        pl.when((z == p.z) & above)(lambda: take(nz))
        pl.when(z > p.z)(lambda: send(z, p.me + 8))
        pl.when(z < p.z)(lambda: send(jnp.where(z == p.z - 1, nz, z), p.me - 8))

    def plane_corner(self):
        p = self.p
        self.w.copy(self.term(3, p.z, self.late), self.in_plane.at[0], self.plane, p.yn).start()

    def plane_sides(self):
        p = self.p
        self.w.copy(self.term(2, p.z, self.late), self.in_plane.at[2], self.plane + 2, p.yn).start()
        ref = self.term(1, p.z, self.late)
        self.add(ref, self.got(self.in_plane.at[0], self.plane))
        self.w.copy(ref, self.in_plane.at[1], self.plane + 1, p.xn).start()

    def plane_own(self):
        ref = self.term(0, self.p.z, self.late)
        self.add(ref, self.got(self.in_plane.at[1], self.plane + 1))
        self.add(ref, self.got(self.in_plane.at[2], self.plane + 2))

    def step(self, kind, number, by_plane):
        p = self.p
        plane, digit = number // 10, number % 10
        takes = (self.send_sib, self.corner, self.take_rest, self.side_x, self.side_y, self.own, self.own_late)
        ends = (self.plane_corner, self.plane_sides, self.plane_own)
        if kind >= len(takes):
            end = ends[kind - len(takes)]
            return (lambda: pl.when(p.z == plane)(end)) if by_plane else end
        take = takes[kind]
        if not by_plane:
            return lambda: p.level(digit, take)
        if take in (self.own, self.own_late):
            return lambda: pl.when((p.z == plane - digit) | (p.z == plane + digit))(lambda: take(plane))
        return lambda: take(plane)

    def drain(self):
        p, nz = self.p, self.p.nz

        def sent(ref, number):
            self.w.copy(ref, ref, number, p.sib).wait_send()

        for i in range(3):
            sent(self.in_plane.at[i], self.plane + i)

        def one(z, carry):
            for column in range(4):
                k = self.slot(column, z)
                sent(self.side.at[k], self.sib + k)
            sent(self.in_first.at[z], self.d1 + z)
            sent(self.in_second.at[z], self.d2 + z)
            sent(self.in_x.at[z], self.xs + z)
            sent(self.in_y.at[z], self.ys + z)

            def lines(slot):
                sent(self.in_line.at[slot], self.line + slot)
                for column in range(4):
                    at = column * (nz + 1) + slot
                    sent(self.in_late.at[at], self.late_line + at)

            pl.when(z > p.z)(lambda: lines(z))
            pl.when(z < p.z)(lambda: lines(jnp.where(z == p.z - 1, nz, z)))
            return carry

        lax.fori_loop(0, nz, one, 0)


def scatter_count(nz):
    return 4 * nz + 4 * nz + nz + 1 + 4 * (nz + 1) + 3


def build_masks(plan, ids_ref, len_ref, key_add, query_one):
    for r in range(plan.rows):
        ids = jnp.broadcast_to(ids_ref[r : r + 1, :], (LANES, SLOTS))
        label = lax.broadcasted_iota(jnp.int32, (LANES, SLOTS), 0)
        place = lax.broadcasted_iota(jnp.int32, (LANES, SLOTS), 1)
        start = jnp.sum((ids < label).astype(F32), axis=1, keepdims=True)
        lengths = len_ref[r]
        lengths = lengths[0:1, :] + lengths[1:2, :]
        live = jnp.zeros((LANES, SLOTS), jnp.int32)
        for j in range(PAIRS):
            live = jnp.where(label == j, lengths[:, j : j + 1], live)
        same = ids == label
        ok = same & (place.astype(F32) - start < live.astype(F32))
        rs = pl.ds(r * SLOTS, SLOTS)
        key_add[rs, :] = jnp.where(ok | (label >= PAIRS), 0.0, -1e30).T.astype(BF16)
        query_one[rs, :] = same.astype(F32).T.astype(BF16)


def split_heads(v):
    lane = lax.broadcasted_iota(jnp.int32, v.shape, 1)
    zero = jnp.zeros_like(v)
    return jnp.concatenate(
        [jnp.where(lane < HEAD_DIM, v, zero), jnp.where(lane < HEAD_DIM, zero, v)], axis=0
    )


def join_heads(v):
    lane = lax.broadcasted_iota(jnp.int32, (SLOTS, LANES), 1)
    return jnp.where(lane < HEAD_DIM, v[:SLOTS], v[SLOTS:])


def head_pair(i, rows):
    r, p = lax.rem(i, rows), i // rows
    return (
        pl.ds(pl.multiple_of(r * SLOTS, 16), SLOTS),
        pl.ds(pl.multiple_of(p * LANES, LANES), LANES),
    )


def scores_of(rs, cs, qkv, key_add, query_one):
    q, k, one = qkv[0, rs, cs], qkv[1, rs, cs], query_one[rs, :]
    q_side = jnp.concatenate([split_heads(q), jnp.concatenate([one, one], axis=0)], axis=1)
    k_side = jnp.concatenate([k, key_add[rs, :]], axis=1)
    return dot_nt(k_side, q_side), q, k


def attend(i, rows, qkv, key_add, query_one, context, log_totals):
    rs, cs = head_pair(i, rows)
    scores, _, _ = scores_of(rs, cs, qkv, key_add, query_one)
    top = jnp.max(scores, axis=0, keepdims=True)
    raised = jnp.exp(scores - top)
    total = jnp.sum(raised, axis=0, keepdims=True)
    shares = (raised * (1.0 / total)).astype(BF16)
    log_totals[i] = top + jnp.log(total)
    context[rs, cs] = join_heads(dot_tn(shares, qkv[2, rs, cs])).astype(BF16)


def attend_back(i, rows, qkv, key_add, query_one, log_totals, grad_context, grad_qkv):
    rs, cs = head_pair(i, rows)
    scores, q, k = scores_of(rs, cs, qkv, key_add, query_one)
    shares = jnp.exp(scores - log_totals[i])
    grad = split_heads(grad_context[rs, cs])
    grad_shares = dot_nt(qkv[2, rs, cs], grad)
    inner = jnp.sum(shares * grad_shares, axis=0, keepdims=True)
    grad_scores = (shares * (grad_shares - inner)).astype(BF16)
    grad_qkv[2, rs, cs] = dot_nn(shares.astype(BF16), grad).astype(BF16)
    grad_qkv[1, rs, cs] = dot_nn(grad_scores, split_heads(q)).astype(BF16)
    grad_qkv[0, rs, cs] = (join_heads(dot_tn(grad_scores, k)) * 0.125).astype(BF16)


def run_beside(count, body, steps):
    def turn(i, carry):
        body(i)
        for j, some in enumerate(steps):
            if some:

                @pl.when(i == j)
                def _(some=some):
                    for step in some:
                        step()

        return carry

    lax.fori_loop(0, count, turn, 0)


def after(code, steps):
    at = ORDER.index(code) + 1
    out = []
    while at < len(ORDER) and ORDER[at] >= 10000:
        out.append(steps[ORDER[at]])
        at += 1
    return out


def beside(kind, count, steps):
    return [after(kind + i, steps) for i in range(count)]


def run(steps):
    for step in steps:
        step()


def joint_weight(plan, ref, b):
    jr = plan.joint_rows
    return ref[0 : plan.joint_src, b * jr : (b + 1) * jr, :].reshape(D, D)


def out_weight(plan, ref):
    return ref[plan.joint_src : plan.n].reshape(D, D)


def in_weight(plan, ref, c):
    ir = plan.in_rows
    return ref[0 : plan.in_src, pl.ds(pl.multiple_of(c * ir, 16), ir), :].reshape(D, D)


def back_weight(plan, ref, c):
    return ref[back_blocks(plan, c)].reshape(D, D)


def back_blocks(plan, c):
    per = (plan.n - plan.in_src) // 4
    return pl.ds(plan.in_src + c * per, per)


def row_slots(r):
    return pl.ds(pl.multiple_of(r * SLOTS, 16), SLOTS)


def token_tiles(plan, size, fn):
    def one(t, carry):
        fn(pl.ds(pl.multiple_of(t * size, 16), size))
        return carry

    lax.fori_loop(0, plan.tokens // size, one, 0)


def gelu_with_slope(h):
    cdf = 0.5 * (1.0 + lax.erf(h * 0.7071067811865476))
    return h * cdf, cdf + h * jnp.exp(-0.5 * h * h) * 0.3989422804014327


def norm_parts(v):
    centred = v - row_mean(v)
    rstd = lax.rsqrt(row_mean(centred * centred) + NORM_EPS)
    return centred * rstd, rstd


def norm_back(grad, xhat, rstd):
    return rstd * (grad - row_mean(grad) - xhat * row_mean(grad * xhat))


def layer_kernel(plan, *refs):
    (x_in, ids, lens, shard_a, shard_f, out_grad_in) = refs[:6]
    (layer_out, in_grad, attn_grad, ffn_grad, bias_grad, params_far, qkv_far, context_far) = refs[6:14]
    (x, weights, active, slope, terms_f, norm_b, grad_hidden, grad_low, acc, xhat, rstd_first, log_totals, key_add,
     query_one, vec, vec_own, vec_held, joined_a, joined_f, halo_a, halo_f, end_a, end_f, vec_a, vec_b, got_a, got_b,
     got, out_a, out_f, send, recv, vec_send, vec_recv, local) = refs[14:49]
    room_f, room_1, room_2 = refs[49:57], refs[57:65], refs[65:73]
    n, nz, rows = plan.n, plan.nz, plan.rows
    place = Place(plan)
    me = place.me
    wire = Wire(send, recv)
    tail_a, tail_f = plan.tail_a, plan.tail_f
    hub_a, hub_b = plan.at_attn_vec[0], plan.at_bias_in[0]
    va, vf, gap = 5 * D // LANES, 3 * D // LANES, plan.gap
    bits = n.bit_length() - 1
    ra, half = plan.rows_a, D // 2
    jr, ir = plan.joint_rows, plan.in_rows
    per = (n - plan.in_src) // 4
    turns = HEADS // 2 * rows
    cols = [pl.ds(u * LANES, LANES) for u in range(6)]
    params = terms_f.at[:, 0:ra, :]
    qkv, context = slope.at[0:3], slope.at[3]
    out_grad = grad_hidden
    params_back = weights.at[:, 0:ra, :]
    terms_a = weights.at[:, ra : 2 * ra, :]
    qkv_back, context_back = active.at[0:3], active.at[3]
    grad_qkv, grad_context = slope.at[0:3], slope.at[3]

    base = [0]

    def numbers(count):
        base[0] += count
        return base[0] - count

    halo_in, halo_out = numbers(2), numbers(2)
    gather_a = Gather(place, wire, numbers(gather_count(nz)), params, *plan.part_a)
    gather_f = Gather(place, wire, numbers(gather_count(nz)), weights, *plan.part_f)
    scatter_f = Scatter(place, wire, numbers(scatter_count(nz)), terms_f, (0, D), *plan.part_f, room_f)
    scatter_1 = Scatter(place, wire, numbers(scatter_count(nz)), weights, (0, half), ra, *plan.part_a[1:], room_1)
    scatter_2 = Scatter(place, wire, numbers(scatter_count(nz)), weights, (half, half), ra, *plan.part_a[1:], room_2)
    vec_steps = add_over_all(place, wire, numbers(bits), vec_own, vec_held)
    movers = (None, gather_a, gather_f, scatter_f, scatter_1, scatter_2)
    steps = {}
    for code in ORDER:
        family, kind, number = code // 10000, code // 100 % 100, code % 100
        if family == 6:
            steps[code] = vec_steps[number]
        elif family:
            by_plane = () if family < 3 else (family == 3,)
            steps[code] = movers[family].step(kind, number, *by_plane)

    copies = {}

    def copy_here(name, src, dst):
        copies[name] = pltpu.make_async_copy(src, dst, local.at[len(copies)])

    copy_here("x", x_in, x)
    copy_here("out_grad", out_grad_in, out_grad)
    copy_here("params", params, params_far)
    copy_here("qkv", qkv, qkv_far)
    copy_here("context", context, context_far)
    copy_here("result", out_grad, layer_out)
    copy_here("params_back", params_far, params_back)
    copy_here("qkv_back", qkv_far, qkv_back)
    copy_here("context_back", context_far, context_back)
    copy_here("in_grad", acc, in_grad)
    entered = place.greet((hub_a, hub_b))
    copies["x"].start()
    copies["out_grad"].start()

    joined_a[tail_a : tail_a + plan.unit_a, :] = shard_a[...].astype(F32)
    joined_f[tail_f : tail_f + plan.unit_f, :] = shard_f[...].astype(F32)
    end_a[...] = joined_a[plan.unit_a : plan.unit_a + tail_a, :]
    end_f[...] = joined_f[plan.unit_f : plan.unit_f + tail_f, :]
    at = tail_a + plan.at_attn_vec[1]
    vec_a[0:va, :] = joined_a[at : at + va, :].astype(BF16)
    at = tail_f + plan.at_ffn_vec[1]
    vec_a[va : va + vf, :] = joined_f[at : at + vf, :].astype(BF16)
    at = tail_f + plan.at_bias_in[1]
    vec_b[...] = jnp.zeros_like(vec_b)
    vec_b[0:gap, :] = joined_f[at : at + gap, :].astype(BF16)
    entered()

    @pl.when(me < n - 1)
    def _():
        wire.copy(end_a, halo_a, halo_in, me + 1).start()
        wire.copy(end_f, halo_f, halo_in + 1, me + 1).start()

    def vec_copy(src, dst, which, partner):
        return pltpu.make_async_remote_copy(
            src_ref=src, dst_ref=dst, send_sem=vec_send.at[partner], recv_sem=vec_recv.at[which],
            device_id=(partner,), device_id_type=MESH,
        )

    def to_all(src, dst, which, fn):
        @pl.when(me == (hub_a, hub_b)[which])
        def _():
            def one(j, carry):
                pl.when(j != me)(lambda: fn(vec_copy(src, dst, which, j)))
                return carry

            lax.fori_loop(0, n, one, 0)

    to_all(vec_a, got_a, 0, lambda copy: copy.start())
    to_all(vec_b, got_b, 1, lambda copy: copy.start())

    @pl.when(me > 0)
    def _():
        wire.copy(end_a, halo_a, halo_in, me - 1).wait_recv()
        joined_a[0:tail_a, :] = halo_a[...]

    start = tail_a - plan.shift_a(me)
    mine = params.at[me]

    @pl.when(me < plan.joint_src)
    def _():
        for b in range(3):
            for u in range(6):
                mine[b * jr : (b + 1) * jr, cols[u]] = joined_a[
                    pl.ds(start + 6 * b + u, jr, stride=18), :
                ].astype(BF16)

    @pl.when(me >= plan.joint_src)
    def _():
        for u in range(6):
            mine[:, cols[u]] = joined_a[pl.ds(start + u, ra, stride=6), :].astype(BF16)

    run([steps[code] for code in ORDER[: ORDER.index(RELAY)]])

    @pl.when(me > 0)
    def _():
        wire.copy(end_f, halo_f, halo_in + 1, me - 1).wait_recv()
        joined_f[0:tail_f, :] = halo_f[...]

    start_f = tail_f - plan.shift_f(me)
    mine_f = weights.at[me]

    @pl.when(me < plan.in_src)
    def _():
        for c in range(4):
            for u in range(6):
                mine_f[c * ir : (c + 1) * ir, cols[u]] = joined_f[
                    pl.ds(start_f + 6 * c + u, ir, stride=24), :
                ].astype(BF16)

    @pl.when(me >= plan.in_src)
    def _():
        for u in range(6):
            mine_f[:, cols[u]] = joined_f[pl.ds(start_f + u, plan.rows_f, stride=6), :].astype(BF16)

    run(after(RELAY, steps))
    build_masks(plan, ids, lens, key_add, query_one)

    @pl.when(me == hub_a)
    def _():
        got_a[...] = vec_a[...]

    @pl.when(me == hub_b)
    def _():
        got_b[...] = vec_b[...]

    @pl.when(me != hub_a)
    def _():
        vec_copy(vec_a, got_a, 0, hub_a).wait_recv()

    @pl.when(me != hub_b)
    def _():
        vec_copy(vec_b, got_b, 1, hub_b).wait_recv()

    got[0 : va + vf, :] = got_a[0 : va + vf, :].astype(F32)
    got[va + vf : va + vf + gap, :] = got_b[0:gap, :].astype(F32)
    vec[...] = jnp.zeros_like(vec)
    for u in range(6):
        vec[0:5, cols[u]] = got[pl.ds(u, 5, stride=6), :]
        vec[9:12, cols[u]] = got[pl.ds(va + u, 3, stride=6), :]
        vec[5:9, cols[u]] = got[pl.ds(va + vf + u, 4, stride=6), :]

    copies["x"].wait()
    scale = jnp.asarray(HEAD_DIM ** (-0.5), BF16)
    held = D // (nz - 1)
    partial = (acc, xhat)
    project = [code for code in ORDER if PROJECT <= code < PROJECT + nz]
    for j, code in enumerate(project):
        z = code - PROJECT
        if z < nz - 1:
            blocks, columns = pl.ds(8 * z, 8), pl.ds(held * z, held)
            for b in range(2):
                now = dot_nn(x[:, columns], params[blocks, b * jr : (b + 1) * jr, :].reshape(held, D))
                if j > 0:
                    now = now + partial[b][...]
                if j < nz - 2:
                    partial[b][...] = now
                elif b == 0:
                    qkv[0] = (now + vec[0:1, :]).astype(BF16) * scale
                else:
                    qkv[1] = now.astype(BF16)
        else:
            qkv[2] = (dot_nn(x[...], joint_weight(plan, params, 2)) + vec[1:2, :]).astype(BF16)
        run(after(code, steps))
    copies["qkv"].start()
    pairs = turns // rows

    def attend_pair(i):
        for r in range(rows):
            attend(i * rows + r, rows, qkv, key_add, query_one, context, log_totals)

    run_beside(pairs, attend_pair, beside(ATTEND, pairs, steps))
    copies["params"].start()
    copies["context"].start()
    gain_first, shift_first, bias_back = vec[3:4, :], vec[4:5, :], vec[9:10, :]
    gain_second, shift_second = vec[10:11, :], vec[11:12, :]

    def norm(t):
        rs = row_slots(t)
        v = x[rs, :].astype(F32) + (dot_nn(context[rs, :], out_weight(plan, params)) + vec[2:3, :])
        now, rstd = norm_parts(v)
        xhat[rs, :] = now
        rstd_first[rs, :] = jnp.broadcast_to(rstd, (rstd.shape[0], LANES))
        v = now * gain_first + shift_first
        norm_b[rs, :] = v.astype(BF16)
        acc[rs, :] = v + bias_back

    run_beside(rows, norm, beside(NORM, rows, steps))

    copies["qkv"].wait()
    copies["context"].wait()

    def up(c):
        hidden = dot_nn(norm_b[...], in_weight(plan, weights, c)) + vec[pl.ds(5 + c, 1), :]
        value, incline = gelu_with_slope(hidden)
        active[c] = value.astype(BF16)
        slope[c] = incline.astype(BF16)

    run_beside(4, up, beside(UP, 4, steps))

    def down(c):
        acc[...] += dot_nn(active[c], back_weight(plan, weights, c))

    run_beside(4, down, beside(DOWN, 4, steps))
    copies["out_grad"].wait()
    grads = vec_own.at[0]
    grads[...] = jnp.zeros(grads.shape, F32)

    def turn(rs):
        now, rstd = norm_parts(acc[rs, :])
        cot = out_grad[rs, :].astype(F32)
        out_grad[rs, :] = (now * gain_second + shift_second).astype(BF16)
        grads[10:11, :] += col_sum(cot * now)
        grads[11:12, :] += col_sum(cot)
        grad = norm_back(cot * gain_second, now, rstd)
        acc[rs, :] = grad
        low = grad.astype(BF16)
        grad_low[rs, :] = low
        grads[9:10, :] += col_sum(low.astype(F32))

    token_tiles(plan, SLOTS, turn)
    copies["result"].start()
    copies["params"].wait()
    gather_a.drain()

    back_order = (2, 3, 0, 1)
    for c in back_order:
        terms_f[back_blocks(plan, c)] = (
            dot_tn(active[c], grad_low[...]).astype(BF16).reshape(per, plan.rows_f, D)
        )
        if c == back_order[1]:
            run(after(BACK_WEIGHT, steps))
    run(after(BACK_WEIGHT + 1, steps))
    copies["context_back"].start()
    copies["qkv_back"].start()
    copies["result"].wait()

    def hidden_back(i):
        c = i // 2

        @pl.when(i == 2 * c)
        def _():
            into_hidden = dot_nt(grad_low[...], back_weight(plan, weights, c))
            grad = (slope[c].astype(F32) * into_hidden).astype(BF16)
            grad_hidden[...] = grad
            grads[pl.ds(5 + c, 1), :] += col_sum(grad.astype(F32))
            acc[...] += dot_nt(grad, in_weight(plan, weights, c))

        @pl.when(i != 2 * c)
        def _():
            in_rows = pl.ds(pl.multiple_of(c * ir, 16), ir)
            terms_f[0 : plan.in_src, in_rows, :] = (
                dot_tn(norm_b[...], grad_hidden[...]).astype(BF16).reshape(plan.in_src, ir, D)
            )

    run_beside(8, hidden_back, beside(HIDDEN, 8, steps))
    gather_f.drain()
    copies["params_back"].start()

    def leave(rs):
        grad, now = acc[rs, :], xhat[rs, :]
        grads[3:4, :] += col_sum(grad * now)
        grads[4:5, :] += col_sum(grad)
        grad = norm_back(grad * gain_first, now, rstd_first[rs, 0:1])
        acc[rs, :] = grad
        grad = grad.astype(BF16)
        grad_low[rs, :] = grad
        grads[2:3, :] += col_sum(grad.astype(F32))

    token_tiles(plan, SLOTS, leave)
    run(after(LEAVE, steps))
    copies["params_back"].wait()

    def into_context(rs):
        grad_context[rs, :] = dot_nt(grad_low[rs, :], out_weight(plan, params_back)).astype(BF16)

    token_tiles(plan, SLOTS, into_context)
    run(after(LEAVE + 1, steps))
    copies["context_back"].wait()
    terms_a[plan.joint_src : n] = (
        dot_tn(context_back[...], grad_low[...]).astype(BF16).reshape(n - plan.joint_src, ra, D)
    )
    copies["qkv_back"].wait()
    run(after(LEAVE + 2, steps))

    def joint_terms(first):
        for b in range(3):
            terms_a[0 : plan.joint_src, b * jr : (b + 1) * jr, first : first + half] = (
                dot_tn(x[...], grad_qkv[b, :, first : first + half]).astype(BF16).reshape(plan.joint_src, jr, half)
            )

    def back_pair(i):
        for r in range(rows):
            attend_back(i * rows + r, rows, qkv_back, key_add, query_one, log_totals, grad_context, grad_qkv)

    beside_back = beside(ATTEND_BACK, pairs, steps)
    beside_back[pairs // 2 - 1] += [lambda: joint_terms(0)] + after(JOINT + 1, steps)
    run_beside(pairs, back_pair, beside_back)
    joint_terms(half)
    grads[0:1, :] = col_sum(grad_qkv[0].astype(F32))
    grads[1:2, :] = col_sum(grad_qkv[2].astype(F32))
    run(after(JOINT + 2, steps))

    def input_grad(rs):
        now = acc[rs, :]
        for b in range(3):
            now = now + dot_nt(grad_qkv[b, rs, :], joint_weight(plan, params_back, b))
        acc[rs, :] = now

    size = plan.tokens // 4
    for j in range(4):
        input_grad(pl.ds(j * size, size))
        if j == 3:
            copies["in_grad"].start()
        run(after(INPUT_GRAD + j, steps))

    summed = vec_own.at[bits]
    total_f, total_a = terms_f.at[me], terms_a.at[me]

    @pl.when(me < plan.in_src)
    def _():
        for c in range(4):
            for u in range(6):
                joined_f[pl.ds(6 * c + u, ir, stride=24), :] = total_f[c * ir : (c + 1) * ir, cols[u]].astype(F32)

    @pl.when(me >= plan.in_src)
    def _():
        for u in range(6):
            joined_f[pl.ds(u, plan.rows_f, stride=6), :] = total_f[:, cols[u]].astype(F32)

    @pl.when(me < plan.joint_src)
    def _():
        for b in range(3):
            for u in range(6):
                joined_a[pl.ds(6 * b + u, jr, stride=18), :] = total_a[b * jr : (b + 1) * jr, cols[u]].astype(F32)

    @pl.when(me >= plan.joint_src)
    def _():
        for u in range(6):
            joined_a[pl.ds(u, ra, stride=6), :] = total_a[:, cols[u]].astype(F32)

    head_a, head_f = joined_a.at[0:tail_a], joined_f.at[0:tail_f]

    @pl.when(me > 0)
    def _():
        wire.copy(head_f, out_f, halo_out + 1, me - 1).start()
        wire.copy(head_a, out_a, halo_out, me - 1).start()

    rest_a = pl.ds(plan.block_a, tail_a)
    rest_f = pl.ds(plan.block_f, tail_f)

    @pl.when(me < n - 1)
    def _():
        wire.copy(head_f, out_f, halo_out + 1, me + 1).wait_recv()
        wire.copy(head_a, out_a, halo_out, me + 1).wait_recv()
        joined_f[rest_f, :] = out_f[...]
        joined_a[rest_a, :] = out_a[...]

    @pl.when(me == hub_b)
    def _():
        for u in range(6):
            joined_f[pl.ds(plan.block_f + u, 4, stride=6), :] = summed[5:9, cols[u]]
        joined_f[plan.block_f + gap : plan.block_f + tail_f, :] = out_f[0 : tail_f - gap, :]

    @pl.when(me == n - 1)
    def _():
        joined_f[rest_f, :] = jnp.zeros((tail_f, LANES), F32)
        joined_a[rest_a, :] = jnp.zeros((tail_a, LANES), F32)
        for u in range(6):
            joined_f[pl.ds(plan.block_f + u, 3, stride=6), :] = summed[9:12, cols[u]]
            joined_a[pl.ds(plan.block_a + u, 5, stride=6), :] = summed[0:5, cols[u]]

    ffn_grad[...] = joined_f[pl.ds(plan.shift_f(me), plan.unit_f), :]
    attn_grad[...] = joined_a[pl.ds(plan.shift_a(me), plan.unit_a), :]
    for u in range(6):
        bias_grad[u : u + 1, :] = summed[2:3, cols[u]]
    copies["in_grad"].wait()
    for mover in (scatter_f, scatter_1, scatter_2):
        mover.drain()
    to_all(vec_a, got_a, 0, lambda copy: copy.wait_send())
    to_all(vec_b, got_b, 1, lambda copy: copy.wait_send())

    @pl.when(me < n - 1)
    def _():
        wire.copy(end_a, halo_a, halo_in, me + 1).wait_send()
        wire.copy(end_f, halo_f, halo_in + 1, me + 1).wait_send()

    @pl.when(me > 0)
    def _():
        wire.copy(head_f, out_f, halo_out + 1, me - 1).wait_send()
        wire.copy(head_a, out_a, halo_out, me - 1).wait_send()


def hand_over(*arrays):
    def kernel(*refs):
        for j in range(len(arrays)):
            refs[len(arrays) + j][...] = refs[j][...]

    parts = 4
    specs = []
    for array in arrays:
        count, width = array.shape
        if count % (16 * parts) == 0:
            specs.append(pl.BlockSpec((count // parts, width), lambda i: (i, 0)))
        else:
            specs.append(pl.BlockSpec((count, width), lambda i: (0, 0)))
    return pl.pallas_call(
        kernel,
        name="hand_over",
        grid=(parts,),
        out_shape=[jax.ShapeDtypeStruct(array.shape, array.dtype) for array in arrays],
        in_specs=specs,
        out_specs=specs,
    )(*arrays)


def fused_body(plan, layer_in, pair_ids, pair_lengths, attn_shard, ffn_shard, out_grad):
    n, t, nz = plan.n, plan.tokens, plan.nz
    shape = jax.ShapeDtypeStruct
    bits = n.bit_length() - 1
    turns = HEADS // 2 * plan.rows
    sems = 4 + bits + 2 * gather_count(nz) + 3 * scatter_count(nz)
    low, full = pltpu.VMEM((t, D), BF16), pltpu.VMEM((t, D), F32)
    blocks = pltpu.VMEM((n, plan.rows_f, D), BF16)
    wide = pltpu.VMEM((4, t, D), BF16)
    side = pltpu.VMEM((t, LANES), BF16)
    vmem, far = pl.BlockSpec(memory_space=pltpu.VMEM), pl.BlockSpec(memory_space=pl.ANY)

    def units(count):
        return pltpu.VMEM((count, LANES), F32)

    def low_units(count):
        return pltpu.VMEM((count, LANES), BF16)

    layer_out, in_grad, attn_grad, ffn_grad, bias_grad = pl.pallas_call(
        functools.partial(layer_kernel, plan),
        name="layer",
        out_shape=[
            shape((t, D), BF16),
            shape((t, D), F32),
            shape((plan.unit_a, LANES), F32),
            shape((plan.unit_f, LANES), F32),
            shape((D // LANES, LANES), F32),
            shape((n, plan.rows_a, D), BF16),
            shape((3, t, D), BF16),
            shape((t, D), BF16),
        ],
        in_specs=[far] + [vmem] * 4 + [far],
        out_specs=[far] * 2 + [vmem] * 3 + [far] * 3,
        scratch_shapes=[
            low, blocks, wide, wide, blocks, low, low, low, full, full,
            pltpu.VMEM((t, LANES), F32),
            pltpu.VMEM((turns, 1, 2 * SLOTS), F32),
            side, side,
            pltpu.VMEM((16, D), F32),
            pltpu.VMEM((bits + 1, 16, D), F32),
            pltpu.VMEM((bits, 16, D), F32),
            units(plan.tail_a + -(-plan.unit_a // 8) * 8 + 8),
            units(plan.tail_f + -(-plan.unit_f // 8) * 8 + 8),
            units(plan.tail_a), units(plan.tail_f), units(plan.tail_a), units(plan.tail_f),
            low_units(48), low_units(32), low_units(48), low_units(32),
            units(80), units(plan.tail_a), units(plan.tail_f),
            pltpu.SemaphoreType.DMA((sems,)),
            pltpu.SemaphoreType.DMA((sems,)),
            pltpu.SemaphoreType.DMA((n,)),
            pltpu.SemaphoreType.DMA((2,)),
            pltpu.SemaphoreType.DMA((12,)),
        ]
        + Scatter.rooms(nz, D, *plan.part_f)
        + Scatter.rooms(nz, D // 2, *plan.part_a)
        + Scatter.rooms(nz, D // 2, *plan.part_a),
        compiler_params=pltpu.CompilerParams(
            collective_id=0, has_side_effects=True, vmem_limit_bytes=VMEM_LIMIT
        ),
    )(
        layer_in.reshape(t, D),
        pair_ids,
        jnp.swapaxes(pair_lengths, 1, 2),
        attn_shard.reshape(plan.unit_a, LANES),
        ffn_shard.reshape(plan.unit_f, LANES),
        out_grad.reshape(t, D),
    )[:5]
    layer_out, in_grad, attn_grad, ffn_grad, bias_grad = hand_over(layer_out, in_grad, attn_grad, ffn_grad, bias_grad)
    return (
        layer_out.reshape(layer_in.shape),
        in_grad.reshape(layer_in.shape),
        attn_grad.reshape(-1),
        ffn_grad.reshape(-1),
        bias_grad.reshape(-1),
    )


def unpack_attention(flattened):
    offset = 3 * D * D
    weight_joint = flattened[:offset].reshape(D, 3 * D)
    weight_out = flattened[offset : offset + D * D].reshape(D, D)
    offset = offset + D * D
    vectors = flattened[offset : offset + 5 * D].reshape(5, D)
    return (weight_joint, weight_out, vectors[0], vectors[1], vectors[2], vectors[3], vectors[4])


def unpack_feedforward(flattened):
    offset = D * FF
    weight_in = flattened[:offset].reshape(D, FF)
    bias_in = flattened[offset : offset + FF]
    offset = offset + FF
    weight_back = flattened[offset : offset + FF * D].reshape(FF, D)
    offset = offset + FF * D
    vectors = flattened[offset : offset + 3 * D].reshape(3, D)
    return (weight_in, bias_in, weight_back, vectors[0], vectors[1], vectors[2])


def layer_norm(values, gain_vec, shift_vec):
    row_mean = jnp.mean(values, axis=-1, keepdims=True)
    centred = values - row_mean
    row_var = jnp.mean(centred * centred, axis=-1, keepdims=True)
    return centred * lax.rsqrt(row_var + NORM_EPS) * gain_vec + shift_vec


def exact_gelu(values):
    return jax.nn.gelu(values, approximate=False)


def key_mask(pair_ids, pair_lengths):
    labels = jnp.arange(PAIRS, dtype=jnp.int32)
    member = pair_ids[:, :, None] == labels[None, None, :]
    starts = jnp.sum((pair_ids[:, :, None] < labels[None, None, :]).astype(jnp.int32), axis=1)
    live_len = pair_lengths[:, :, 0] + pair_lengths[:, :, 1]
    slot_start = jnp.sum(jnp.where(member, starts[:, None, :], 0), axis=-1)
    slot_len = jnp.sum(jnp.where(member, live_len[:, None, :], 0), axis=-1)
    places = jnp.arange(pair_ids.shape[1], dtype=jnp.int32)[None, :]
    is_live = places - slot_start < slot_len
    return (pair_ids[:, :, None] == pair_ids[:, None, :]) & is_live[:, None, :]


def contract_rows(one_side, other_side):
    return lax.dot_general(
        one_side, other_side, (((0,), (0,)), ((), ())), preferred_element_type=jnp.float32
    )


def contract_cols(one_side, other_side):
    return lax.dot_general(
        one_side, other_side, (((1,), (1,)), ((), ())), preferred_element_type=jnp.float32
    )


def attend_forward(queries, key_rows, value_rows, key_ok, score_scale):

    def head_block(block_index):
        head_start = block_index * 4
        query_b = lax.dynamic_slice_in_dim(queries, head_start, 4, 2)
        key_b = lax.dynamic_slice_in_dim(key_rows, head_start, 4, 2)
        value_b = lax.dynamic_slice_in_dim(value_rows, head_start, 4, 2)
        scores = (
            jnp.einsum("rqhd,rkhd->rhqk", query_b, key_b, preferred_element_type=jnp.float32)
            * score_scale
        )
        scores = jnp.where(key_ok[:, None], scores, -1e30)
        row_max = jnp.max(scores, axis=-1, keepdims=True)
        raised = jnp.exp(scores - row_max)
        totals = jnp.sum(raised, axis=-1, keepdims=True)
        shares = (raised / totals).astype(jnp.bfloat16)
        context = jnp.einsum("rhqk,rkhd->rqhd", shares, value_b, preferred_element_type=jnp.float32)
        return (context, row_max + jnp.log(totals))

    return lax.map(head_block, jnp.arange(HEADS // 4))


def attend_backward(queries, key_rows, value_rows, grad_context, log_totals, key_ok, score_scale):

    def head_block(operands):
        block_index, log_total = operands
        head_start = block_index * 4
        query_b = lax.dynamic_slice_in_dim(queries, head_start, 4, 2)
        key_b = lax.dynamic_slice_in_dim(key_rows, head_start, 4, 2)
        value_b = lax.dynamic_slice_in_dim(value_rows, head_start, 4, 2)
        grad_block = lax.dynamic_slice_in_dim(grad_context, head_start, 4, 2)
        scores = (
            jnp.einsum("rqhd,rkhd->rhqk", query_b, key_b, preferred_element_type=jnp.float32)
            * score_scale
        )
        shares = jnp.where(key_ok[:, None], jnp.exp(scores - log_total), 0.0)
        grad_shares = jnp.einsum(
            "rqhd,rkhd->rhqk", grad_block, value_b, preferred_element_type=jnp.float32
        )
        inner_sum = jnp.sum(shares * grad_shares, axis=-1, keepdims=True)
        grad_scores = (shares * (grad_shares - inner_sum)).astype(jnp.bfloat16)
        grad_query = (
            jnp.einsum("rhqk,rkhd->rqhd", grad_scores, key_b, preferred_element_type=jnp.float32)
            * score_scale
        )
        grad_key = (
            jnp.einsum("rhqk,rqhd->rkhd", grad_scores, query_b, preferred_element_type=jnp.float32)
            * score_scale
        )
        grad_value = jnp.einsum(
            "rhqk,rqhd->rkhd",
            shares.astype(jnp.bfloat16),
            grad_block,
            preferred_element_type=jnp.float32,
        )
        return (grad_query, grad_key, grad_value)

    gradients = lax.map(head_block, (jnp.arange(HEADS // 4), log_totals))
    return [jnp.moveaxis(piece, 0, 2).reshape(-1, D) for piece in gradients]


def plain_body(layer_in, pair_ids, pair_lengths, attn_shard, ffn_shard, out_grad):
    row_count = layer_in.shape[0]
    tokens = row_count * SLOTS
    score_scale = HEAD_DIM ** (-0.5)
    key_ok = key_mask(pair_ids, pair_lengths)
    att_whole = lax.all_gather(attn_shard, "fsdp", axis=0, tiled=True)
    weight_joint, weight_out, bias_query, bias_value, bias_out, gain_first, shift_first = (
        unpack_attention(att_whole)
    )
    inputs = layer_in.reshape(tokens, D)
    bias_joint = jnp.concatenate([bias_query, jnp.zeros_like(bias_query), bias_value]).astype(
        jnp.float32
    )
    projected = (
        jnp.dot(inputs, weight_joint, preferred_element_type=jnp.float32) + bias_joint
    ).astype(jnp.bfloat16)
    projected = projected.reshape(row_count, SLOTS, 3, HEADS, HEAD_DIM)
    queries = projected[:, :, 0]
    key_rows = projected[:, :, 1]
    value_rows = projected[:, :, 2]
    contexts, log_totals = attend_forward(queries, key_rows, value_rows, key_ok, score_scale)
    context = jnp.moveaxis(contexts, 0, 2).reshape(tokens, D).astype(jnp.bfloat16)
    attn_out = jnp.dot(context, weight_out, preferred_element_type=jnp.float32) + bias_out.astype(
        jnp.float32
    )
    norm_first, first_pull = jax.vjp(
        layer_norm,
        inputs.astype(jnp.float32) + attn_out,
        gain_first.astype(jnp.float32),
        shift_first.astype(jnp.float32),
    )
    norm_first_b = norm_first.astype(jnp.bfloat16)
    feed_whole = lax.all_gather(ffn_shard, "fsdp", axis=0, tiled=True)
    weight_in, bias_in, weight_back, bias_back, gain_second, shift_second = unpack_feedforward(
        feed_whole
    )
    hidden = jnp.dot(norm_first_b, weight_in, preferred_element_type=jnp.float32) + bias_in.astype(
        jnp.float32
    )
    active, gelu_pull = jax.vjp(exact_gelu, hidden)
    active_b = active.astype(jnp.bfloat16)
    ffn_out = jnp.dot(active_b, weight_back, preferred_element_type=jnp.float32) + bias_back.astype(
        jnp.float32
    )
    result, second_pull = jax.vjp(
        layer_norm,
        norm_first + ffn_out,
        gain_second.astype(jnp.float32),
        shift_second.astype(jnp.float32),
    )
    layer_out = result.astype(jnp.bfloat16).reshape(row_count, SLOTS, D)
    feed_back = lax.all_gather(ffn_shard, "fsdp", axis=0, tiled=True)
    weight_in, bias_in, weight_back, bias_back, gain_second, shift_second = unpack_feedforward(
        feed_back
    )
    cotangent = out_grad.reshape(tokens, D).astype(jnp.float32)
    grad_sum_second, grad_gain_second, grad_shift_second = second_pull(cotangent)
    grad_ffn = grad_sum_second.astype(jnp.bfloat16)
    grad_bias_back = jnp.sum(grad_ffn.astype(jnp.float32), axis=0)
    grad_weight_back = contract_rows(active_b, grad_ffn)
    (grad_hidden,) = gelu_pull(contract_cols(grad_ffn, weight_back))
    grad_hidden = grad_hidden.astype(jnp.bfloat16)
    grad_bias_in = jnp.sum(grad_hidden.astype(jnp.float32), axis=0)
    grad_weight_in = contract_rows(norm_first_b, grad_hidden)
    grad_norm_first = grad_sum_second + contract_cols(grad_hidden, weight_in)
    grad_sum_first, grad_gain_first, grad_shift_first = first_pull(grad_norm_first)
    feed_pad = feed_back.shape[0] - (2 * D * FF + FF + 3 * D)
    feed_full = jnp.concatenate(
        [
            grad_weight_in.reshape(-1),
            grad_bias_in,
            grad_weight_back.reshape(-1),
            grad_bias_back,
            grad_gain_second,
            grad_shift_second,
            jnp.zeros((feed_pad,), jnp.float32),
        ]
    )
    ffn_grad = lax.psum_scatter(feed_full, "fsdp", scatter_dimension=0, tiled=True)
    att_back = lax.all_gather(attn_shard, "fsdp", axis=0, tiled=True)
    weight_joint, weight_out, bias_query, bias_value, bias_out, gain_first, shift_first = (
        unpack_attention(att_back)
    )
    grad_attn = grad_sum_first.astype(jnp.bfloat16)
    grad_bias_out = jnp.sum(grad_attn.astype(jnp.float32), axis=0)
    out_bias_grad = lax.psum(grad_bias_out, "fsdp")
    grad_weight_out = contract_rows(context, grad_attn)
    grad_context = (
        contract_cols(grad_attn, weight_out)
        .astype(jnp.bfloat16)
        .reshape(row_count, SLOTS, HEADS, HEAD_DIM)
    )
    grad_query, grad_key, grad_value = attend_backward(
        queries, key_rows, value_rows, grad_context, log_totals, key_ok, score_scale
    )
    grad_projected = jnp.concatenate([grad_query, grad_key, grad_value], axis=-1).astype(
        jnp.bfloat16
    )
    column_sums = jnp.sum(grad_projected.astype(jnp.float32), axis=0)
    grad_weight_joint = contract_rows(inputs, grad_projected)
    in_grad = grad_sum_first + contract_cols(grad_projected, weight_joint)
    att_pad = att_back.shape[0] - (4 * D * D + 5 * D)
    attn_full = jnp.concatenate(
        [
            grad_weight_joint.reshape(-1),
            grad_weight_out.reshape(-1),
            column_sums[:D],
            column_sums[2 * D :],
            grad_bias_out,
            grad_gain_first,
            grad_shift_first,
            jnp.zeros((att_pad,), jnp.float32),
        ]
    )
    attn_grad = lax.psum_scatter(attn_full, "fsdp", scatter_dimension=0, tiled=True)
    return (layer_out, in_grad.reshape(row_count, SLOTS, D), attn_grad, ffn_grad, out_bias_grad)


def body(layer_in, pair_ids, pair_lengths, attn_shard, ffn_shard, out_grad, devices):
    plan = Plan(devices, attn_shard.shape[0], ffn_shard.shape[0], layer_in.shape[0])
    run = functools.partial(fused_body, plan) if plan.fits() else plain_body
    return run(layer_in, pair_ids, pair_lengths, attn_shard, ffn_shard, out_grad)


def solution(mesh):
    placed = (
        P("fsdp", None, None),
        P("fsdp", None),
        P("fsdp", None, None),
        P("fsdp"),
        P("fsdp"),
        P("fsdp", None, None),
    )
    return jax.shard_map(
        functools.partial(body, devices=mesh.shape["fsdp"]),
        mesh=mesh,
        in_specs=placed,
        out_specs=(P("fsdp", None, None), P("fsdp", None, None), P("fsdp"), P("fsdp"), P()),
        check_vma=False,
    )
```

profile of v0, /device:TPU:1, one launch (start us, length us, event | category | flops | bytes accessed | tf_op | source)
XLA Modules:
  0.0 163.6 jit_solution(231520647152381992)
XLA Ops:
  0.6 157.5 %layer.1 = (bf16[832,768]{1,0:T(8,128)(2,1)}, f32[832,768]{1,0:T(8,128)}, f32[577,128]{1,0:T(8,128)}, f32[1154,128]{1,0:T(8,128)}, f32[6,128]{1,0:T(8,128)}, /*i...) custom-call(bf16[832,768]{1,0:T(8,128)(2,1)} %bitcast.10, s32[2,416]{1,0:T(2,128)} %refs_1_.1, ...), custom_call_target="tpu_custom_call" | custom-call | tf_op jit(solution)/shard_map/layer/pallas_call | solution.py:1178
  158.2 5.1 %hand_over.1 = (bf16[832,768]{1,0:T(8,128)(2,1)}, f32[832,768]{1,0:T(8,128)}, f32[577,128]{1,0:T(8,128)}, f32[1154,128]{1,0:T(8,128)}, f32[6,128]{1,0:T(8,128)}) custom-call(bf16[832,768]{1,0:T(8,128)(2,1)} %get-tuple-element.15.refs_0_, f32[832,768]{1,0:T(8,128)} %get-tuple-element.16.refs_1_, f32[577,128]{1,0:T(8,128)} %get-tuple-element.17.refs_2_, ...), custom_call_target="tpu_custom_call" | custom-call | tf_op jit(solution)/shard_map/hand_over/pallas_call | solution.py:1150
where the time goes:
time: 167 us; the launch traced here: 164 us
  Pallas kernels  163 us (98%)
    pallas_call x1, Pallas kernels, fused_body(): pl.pallas_call(functools.partial(layer_kernel, plan), name='layer', out_s...  158 us
    pallas_call x1, Pallas kernels, hand_over(): pl.pallas_call(kernel, name='hand_over', grid=(parts,), out_shape=[jax.Sh...  5.14 us

commit v1 on v0

--- a/solution.py
+++ b/solution.py
@@ -606,7 +606,9 @@
     total = jnp.sum(raised, axis=0, keepdims=True)
     shares = (raised * (1.0 / total)).astype(BF16)
     log_totals[i] = top + jnp.log(total)
-    context[rs, cs] = join_heads(dot_tn(shares, qkv[2, rs, cs])).astype(BF16)
+    turned = dot_tn(qkv[2, rs, cs], shares)
+    row = lax.broadcasted_iota(jnp.int32, (LANES, SLOTS), 0)
+    context[rs, cs] = jnp.where(row < HEAD_DIM, turned[:, :SLOTS], turned[:, SLOTS:]).T.astype(BF16)
 
 
 def attend_back(i, rows, qkv, key_add, query_one, log_totals, grad_context, grad_qkv):
@@ -1139,7 +1141,7 @@
         for j in range(len(arrays)):
             refs[len(arrays) + j][...] = refs[j][...]
 
-    parts = 4
+    parts = 2
     specs = []
     for array in arrays:
         count, width = array.shape

time: 167 us -> 166 us (level)
  no operation moved by 1% of the time
where the time goes in v1:
time: 166 us; the launch traced here: 163 us
  Pallas kernels  162 us (98%)
    pallas_call x1, Pallas kernels, fused_body(): pl.pallas_call(functools.partial(layer_kernel, plan), name='layer', out_s...  158 us
    pallas_call x1, Pallas kernels, hand_over(): pl.pallas_call(kernel, name='hand_over', grid=(parts,), out_shape=[jax.Sh...  4.1 us

profile of v1, /device:TPU:1, one launch (start us, length us, event | category | flops | bytes accessed | tf_op | source)
XLA Modules:
  0.0 162.6 jit_solution(13388722918924958318)
XLA Ops:
  0.6 157.5 %layer.1 = (bf16[832,768]{1,0:T(8,128)(2,1)}, f32[832,768]{1,0:T(8,128)}, f32[577,128]{1,0:T(8,128)}, f32[1154,128]{1,0:T(8,128)}, f32[6,128]{1,0:T(8,128)}, /*i...) custom-call(bf16[832,768]{1,0:T(8,128)(2,1)} %bitcast.10, s32[2,416]{1,0:T(2,128)} %refs_1_.1, ...), custom_call_target="tpu_custom_call" | custom-call | tf_op jit(solution)/shard_map/layer/pallas_call | solution.py:1180
  158.2 4.1 %hand_over.1 = (bf16[832,768]{1,0:T(8,128)(2,1)}, f32[832,768]{1,0:T(8,128)}, f32[577,128]{1,0:T(8,128)}, f32[1154,128]{1,0:T(8,128)}, f32[6,128]{1,0:T(8,128)}) custom-call(bf16[832,768]{1,0:T(8,128)(2,1)} %get-tuple-element.15.refs_0_, f32[832,768]{1,0:T(8,128)} %get-tuple-element.16.refs_1_, f32[577,128]{1,0:T(8,128)} %get-tuple-element.17.refs_2_, ...), custom_call_target="tpu_custom_call" | custom-call | tf_op jit(solution)/shard_map/hand_over/pallas_call | solution.py:1152

commit v2 on v1

--- a/solution.py
+++ b/solution.py
@@ -1200,11 +1200,11 @@
             pltpu.VMEM((16, D), F32),
             pltpu.VMEM((bits + 1, 16, D), F32),
             pltpu.VMEM((bits, 16, D), F32),
-            units(plan.tail_a + -(-plan.unit_a // 8) * 8 + 8),
-            units(plan.tail_f + -(-plan.unit_f // 8) * 8 + 8),
+            units(plan.tail_a + -(-plan.unit_a // 8) * 8 + 40),
+            units(plan.tail_f + -(-plan.unit_f // 8) * 8 + 40),
             units(plan.tail_a), units(plan.tail_f), units(plan.tail_a), units(plan.tail_f),
             low_units(48), low_units(32), low_units(48), low_units(32),
-            units(80), units(plan.tail_a), units(plan.tail_f),
+            units(104), units(plan.tail_a), units(plan.tail_f),
             pltpu.SemaphoreType.DMA((sems,)),
             pltpu.SemaphoreType.DMA((sems,)),
             pltpu.SemaphoreType.DMA((n,)),

time: 166 us -> 166 us (level)
  no operation moved by 1% of the time
where the time goes in v2:
time: 166 us; the launch traced here: 163 us
  Pallas kernels  162 us (98%)
    pallas_call x1, Pallas kernels, fused_body(): pl.pallas_call(functools.partial(layer_kernel, plan), name='layer', out_s...  158 us
    pallas_call x1, Pallas kernels, hand_over(): pl.pallas_call(kernel, name='hand_over', grid=(parts,), out_shape=[jax.Sh...  4.1 us

profile of v2, /device:TPU:1, one launch (start us, length us, event | category | flops | bytes accessed | tf_op | source)
XLA Modules:
  0.0 162.6 jit_solution(10065377068458672174)
XLA Ops:
  0.6 157.6 %layer.1 = (bf16[832,768]{1,0:T(8,128)(2,1)}, f32[832,768]{1,0:T(8,128)}, f32[577,128]{1,0:T(8,128)}, f32[1154,128]{1,0:T(8,128)}, f32[6,128]{1,0:T(8,128)}, /*i...) custom-call(bf16[832,768]{1,0:T(8,128)(2,1)} %bitcast.10, s32[2,416]{1,0:T(2,128)} %refs_1_.1, ...), custom_call_target="tpu_custom_call" | custom-call | tf_op jit(solution)/shard_map/layer/pallas_call | solution.py:1180
  158.2 4.1 %hand_over.1 = (bf16[832,768]{1,0:T(8,128)(2,1)}, f32[832,768]{1,0:T(8,128)}, f32[577,128]{1,0:T(8,128)}, f32[1154,128]{1,0:T(8,128)}, f32[6,128]{1,0:T(8,128)}) custom-call(bf16[832,768]{1,0:T(8,128)(2,1)} %get-tuple-element.15.refs_0_, f32[832,768]{1,0:T(8,128)} %get-tuple-element.16.refs_1_, f32[577,128]{1,0:T(8,128)} %get-tuple-element.17.refs_2_, ...), custom_call_target="tpu_custom_call" | custom-call | tf_op jit(solution)/shard_map/hand_over/pallas_call | solution.py:1152
